TPU v7x, 32 devices: a whole 2x2x4 slice. The times are simulated.
32 devices in a mesh: gx: 4 (over x, core), gy: 8 (over z, y).
Axes of the slice: x: 2, y: 2, z: 4, core: 2. Of those that a mesh axis runs over, the one named last changes fastest.
Arguments:
- hidden_in: bfloat16 [2048, 4096], P('gx', 'gy')
- norm_gain: bfloat16 [4096], P('gy'), may hold values from 0.099609375 to 1.8984375
- query_proj: bfloat16 [4096, 4096], P('gx', 'gy')
- kv_proj: bfloat16 [1024, 4096], P(None, 'gy')
- prompt_lengths: int32 [8], replicated, may hold values from 1 to 1024, 2048 in all
- cache_slot: int32 [128], replicated, may hold values from 0 to 127, as said below
Outputs:
- attention: bfloat16 [2048, 4096], P('gy', 'gx')
- kv_cache: bfloat16 [128, 16, 1024], P('gy', None, 'gx')
Inputs may be any that keep to these rules, and one draw needn't show every extreme that they name: `prompt_lengths`: the 8 prompts sum to 2048 tokens; the longest has exactly 1024. `cache_slot`: A permutation of the 128 slots; slot s is held by index s // 16 of gy. The 16 pages of one token block go to any one index at most 2 times, and every index receives exactly 16 pages.
All inputs are finite; a program needn't handle non-finite values.
Results may differ from a plain program's by a relative error of at most 0.0066.
The roundings to bfloat16 on the way count: a program that leaves them out, or rounds other values in their place, can miss the bound.
Values may be sent and summed in bfloat16 or wider, within the bound.
A program may use at most 128 MiB of HBM per device.

v0:
```python
import math

import jax
import jax.numpy as jnp
from jax import lax
from jax.sharding import PartitionSpec as P

D = 4096
H = 32
KVH = 4
HD = 128
PAGES_DEV = 16


epsilon = 1e-06
rope_base = 5000000.0
masked_out = -1e30


def token_places(prompt_lengths, token_index):
    prompt_ends = jnp.cumsum(prompt_lengths)
    prompt_starts = prompt_ends - prompt_lengths
    segment = jnp.sum((token_index[:, None] >= prompt_ends[None, :]).astype(jnp.int32), axis=1)
    chosen = segment[:, None] == jnp.arange(prompt_lengths.shape[0], dtype=jnp.int32)[None, :]
    opening = jnp.sum(jnp.where(chosen, prompt_starts[None, :], 0), axis=1)
    return (segment, token_index - opening)


def rotate(vectors, places):
    half_size = vectors.shape[-1] // 2
    frequency = rope_base ** (-(jnp.arange(half_size, dtype=jnp.float32) * 2.0) / vectors.shape[-1])
    angles = places.astype(jnp.float32)[:, None] * frequency[None, :]
    cos_part = jnp.cos(angles)[:, None, :]
    sin_part = jnp.sin(angles)[:, None, :]
    leading = vectors[..., :half_size]
    trailing = vectors[..., half_size:]
    return jnp.concatenate(
        [leading * cos_part - trailing * sin_part, trailing * cos_part + leading * sin_part],
        axis=-1,
    )


def local(hidden_in, norm_gain, query_proj, kv_proj, prompt_lengths, cache_slot):
    count_gx = lax.axis_size("gx")
    count_gy = lax.axis_size("gy")
    where_gx = lax.axis_index("gx")
    where_gy = lax.axis_index("gy")
    local_rows = hidden_in.shape[0]
    block_tokens = local_rows * count_gx // count_gy
    all_tokens = block_tokens * count_gy
    heads_here = query_proj.shape[0] // HD
    group_size = H // KVH
    share = count_gx // KVH
    kv_head = where_gx * heads_here // group_size
    contract = (((1,), (1,)), ((), ()))
    kv_width = 2 * HD
    kv_start = kv_head * 2 * HD
    kv_rows = lax.dynamic_slice_in_dim(kv_proj, kv_start, kv_width, 0)
    widened = hidden_in.astype(jnp.float32)
    squares = jnp.sum(widened * widened, axis=1)
    totals = lax.psum(squares, "gy")
    normed = (
        widened * lax.rsqrt(totals / D + epsilon)[:, None] * norm_gain.astype(jnp.float32)[None, :]
    ).astype(jnp.bfloat16)
    gathered = lax.all_gather(normed, "gx", axis=0, tiled=True)
    stacked = jnp.concatenate([query_proj, kv_rows], axis=0)
    projected = lax.psum_scatter(
        lax.dot_general(gathered, stacked, contract, preferred_element_type=jnp.float32),
        "gy",
        scatter_dimension=0,
        tiled=True,
    )
    every_index = jnp.arange(all_tokens, dtype=jnp.int32)
    segment_all, place_all = token_places(prompt_lengths, every_index)
    first_query = where_gy * block_tokens
    token_index = first_query + jnp.arange(block_tokens, dtype=jnp.int32)
    segment_own = lax.dynamic_slice_in_dim(segment_all, first_query, block_tokens, 0)
    place_own = lax.dynamic_slice_in_dim(place_all, first_query, block_tokens, 0)
    query_cols = heads_here * HD
    queries = rotate(
        projected[:, :query_cols].reshape(block_tokens, heads_here, HD), place_own
    ).astype(jnp.bfloat16)
    keys = rotate(projected[:, query_cols : query_cols + HD][:, None, :], place_own)[
        :, 0, :
    ].astype(jnp.bfloat16)
    values = projected[:, query_cols + HD :].astype(jnp.bfloat16)
    if share == 2:
        cache_cols = jnp.where(where_gx % 2 == 0, keys, values)
    else:
        cache_cols = jnp.concatenate([keys, values], axis=1)
    score_scale = 1.0 / math.sqrt(HD)
    last_query = first_query + block_tokens - 1
    first_segment = segment_own[0]
    initial = (
        jnp.full((heads_here, block_tokens), masked_out, jnp.float32),
        jnp.zeros((heads_here, block_tokens), jnp.float32),
        jnp.zeros((heads_here, block_tokens, HD), jnp.float32),
    )
    key_piece = lax.all_gather(keys, "gy", axis=0, tiled=True)
    value_piece = lax.all_gather(values, "gy", axis=0, tiled=True)
    block_count = key_piece.shape[0] // block_tokens
    key_blocks = key_piece.reshape(block_count, block_tokens, HD)
    value_blocks = value_piece.reshape(block_count, block_tokens, HD)

    def one_block(current, inputs):
        key_rows, value_rows, offset = inputs
        block_begin = offset * block_tokens
        key_segment = lax.dynamic_slice_in_dim(segment_all, block_begin, block_tokens, 0)
        skipped = jnp.logical_or(
            block_begin > last_query, key_segment[block_tokens - 1] < first_segment
        )

        def compute(previous):
            running_max, running_sum, running_acc = previous
            key_index = block_begin + jnp.arange(block_tokens, dtype=jnp.int32)
            allowed = (key_segment[None, :] == segment_own[:, None]) & (
                key_index[None, :] <= token_index[:, None]
            )
            scores = (
                jnp.einsum("qhd,kd->hqk", queries, key_rows, preferred_element_type=jnp.float32)
                * score_scale
            )
            scores = jnp.where(allowed[None], scores, masked_out)
            new_max = jnp.maximum(running_max, jnp.max(scores, axis=2))
            weights = jnp.where(allowed[None], jnp.exp(scores - new_max[..., None]), 0.0)
            factor = jnp.exp(running_max - new_max)
            new_sum = running_sum * factor + jnp.sum(weights, axis=2)
            update = jnp.einsum(
                "hqk,kd->hqd",
                weights.astype(jnp.bfloat16),
                value_rows,
                preferred_element_type=jnp.float32,
            )
            return (new_max, new_sum, running_acc * factor[..., None] + update)

        return (lax.cond(skipped, lambda previous: previous, compute, current), None)

    offsets = jnp.arange(block_count, dtype=jnp.int32)
    result, unused = lax.scan(one_block, initial, (key_blocks, value_blocks, offsets))
    final_max, final_sum, final_acc = result
    attention = (
        (final_acc / final_sum[..., None])
        .transpose(1, 0, 2)
        .reshape(block_tokens, query_cols)
        .astype(jnp.bfloat16)
    )
    pages_dev = PAGES_DEV
    page_len = block_tokens // pages_dev
    width_cols = cache_cols.shape[1]
    my_pages = cache_cols.reshape(pages_dev, page_len * width_cols)
    capacity = max(1, pages_dev // count_gy)
    slots_all = count_gy * capacity
    owners = (cache_slot // pages_dev).reshape(count_gy, pages_dev)
    page_range = jnp.arange(pages_dev, dtype=jnp.int32)
    earlier = page_range[None, :] < page_range[:, None]
    same_owner = owners[:, :, None] == owners[:, None, :]
    ranks = jnp.sum((same_owner & earlier[None]).astype(jnp.int32), axis=2)
    my_owner = lax.dynamic_index_in_dim(owners, where_gy, 0, keepdims=False)
    my_rank = lax.dynamic_index_in_dim(ranks, where_gy, 0, keepdims=False)
    target = my_owner * capacity + my_rank
    slot_range = jnp.arange(slots_all, dtype=jnp.int32)
    send_map = (slot_range[:, None] == target[None, :]).astype(jnp.bfloat16)
    outgoing = jnp.dot(send_map, my_pages, preferred_element_type=jnp.float32).astype(jnp.bfloat16)
    outgoing = outgoing.reshape(count_gy, capacity * page_len * width_cols)
    incoming = lax.all_to_all(outgoing, "gy", split_axis=0, concat_axis=0, tiled=True)
    wanted = where_gy * pages_dev + page_range
    matches = cache_slot[None, :] == wanted[:, None]
    page_ids = jnp.arange(cache_slot.shape[0], dtype=jnp.int32)
    source_page = jnp.sum(jnp.where(matches, page_ids[None, :], 0), axis=1)
    source_rank = jnp.sum(jnp.where(matches, ranks.reshape(-1)[None, :], 0), axis=1)
    source_slot = source_page // pages_dev * capacity + source_rank
    take_map = (source_slot[:, None] == slot_range[None, :]).astype(jnp.bfloat16)
    cache_block = jnp.dot(
        take_map,
        incoming.reshape(slots_all, page_len * width_cols),
        preferred_element_type=jnp.float32,
    )
    cache_block = cache_block.astype(jnp.bfloat16).reshape(pages_dev, page_len, width_cols)
    return (attention, cache_block)


def solution(mesh):
    return jax.shard_map(
        local,
        mesh=mesh,
        in_specs=(P("gx", "gy"), P("gy"), P("gx", "gy"), P(None, "gy"), P(), P()),
        out_specs=(P("gy", "gx"), P("gy", None, "gx")),
        check_vma=False,
    )
```

profile of v0, /device:TPU:22, one launch (start us, length us, event | category | flops | bytes accessed | tf_op | source)
XLA Modules:
  0.0 378.1 jit_solution(998636625052015730)
XLA Ops:
  7.2 1.4 fusion.25
  8.6 15.2 %psum.7 = f32[512]{0:T(512)S(1)} all-reduce(f32[512]{0:T(512)S(1)} %fusion.25), channel_id=1, replica_groups=mesh['gx'=4,'gy'=8] {'gy'}, use_global_device_ids=true, to_apply=%region_1.2 | all-reduce | flops 512 | bytes 4096 | tf_op jit(solution)/shard_map/psum | solution.py:61
  23.8 0.7 convert_element_type.52
  24.5 2.0 fusion.27
  26.6 25.2 %all-gather.3.cloned.1.call-done = bf16[2048,512]{1,0:T(8,128)(2,1)} async-done(((bf16[512,512]{1,0:T(8,128)(2,1)}), bf16[2048,512]{1,0:T(8,128)(2,1)}) %all-gather.3.cloned.1.call-update) | async-done | bytes 2097168 | tf_op jit(solution)/shard_map/all_gather | solution.py:65
  51.9 7.6 %fusion.21 = f32[2048,1280]{0,1:T(8,128)} fusion(bf16[2048,512]{1,0:T(8,128)(2,1)} %all-gather.3.cloned.1.call-done, bf16[256,512]{1,0:T(8,128)(2,1)S(1)} %constant_dynamic-slice_fusion.2, bf16[1024,512]{1,0:T(8,128)(2,1)S(1)} %copy-done.2), kind=kOutput, calls=%fused_computation.31 | convolution fusion | flops 2686976000 | bytes 13893632 | tf_op jit(solution)/shard_map/dot_general | solution.py:68
  59.5 0.6 copy-done.3
  60.9 0.5 slice.28
  61.9 0.5 multiply_cosine_fusion
  62.4 175.7 %reduce-scatter.2.cloned.1.call-done = f32[256,1280]{0,1:T(8,128)} async-done(((f32[2048,1280]{0,1:T(8,128)}), f32[256,1280]{0,1:T(8,128)}) %reduce-scatter.2.cloned.1.call-update) | async-done | bytes 1310736 | tf_op jit(solution)/shard_map/reduce_scatter | solution.py:67
  238.1 0.9 slice_bitcast_fusion
  239.3 0.9 slice.50
  240.3 30.6 %all_gather.11 = bf16[2048,128]{0,1:T(8,128)(2,1)} all-gather(bf16[256,128]{0,1:T(8,128)(2,1)S(1)} %slice.50), channel_id=1, replica_groups=mesh['gx'=4,'gy'=8] {'gy'}, dimensions={0}, use_global_device_ids=true | all-gather | bytes 589824 | tf_op jit(solution)/shard_map/all_gather | solution.py:100
  270.9 0.6 fusion.46
  272.1 0.5 broadcast.247
  272.6 1.4 reduce.1
  274.0 0.7 reshape.274
  274.8 7.8 %all-to-all-start = ((bf16[8,2,4096]{2,1,0:T(2,128)(2,1)}), bf16[8,2,4096]{2,1,0:T(2,128)(2,1)S(1)}, u32[]{:S(2)}, u32[]{:S(2)}) async-start(bf16[8,2,4096]{2,1,0:T(2,128)(2,1)} %reshape.274), calls=%async_computation.1 | async-start | bytes 262144 | tf_op jit(solution)/shard_map/all_to_all | solution.py:165
  282.6 0.9 fusion.47
  283.4 0.3 copy.48
  283.8 1.4 copy.49
  285.2 32.4 %all-gather = bf16[2048,1,128]{0,2,1:T(8,128)(2,1)} all-gather(bf16[256,1,128]{0,2,1:T(8,128)(2,1)} %get-tuple-element.271), channel_id=2, replica_groups=mesh['gx'=4,'gy'=8] {'gy'}, dimensions={0}, use_global_device_ids=true | all-gather | bytes 589824 | tf_op jit(solution)/shard_map/all_gather | solution.py:99
  317.5 2.0 copy.46
  319.6 2.0 copy.47
  322.3 46.0 %while.15 = (s32[]{:T(128)}, f32[8,256]{1,0:T(8,128)S(1)}, f32[8,256]{1,0:T(8,128)S(1)}, f32[8,256,128]{2,1,0:T(8,128)S(1)}, s32[8]{0:T(128)S(1)}, /*index=5*/s3...) while((s32[]{:T(128)}, f32[8,256]{1,0:T(8,128)S(1)}, ...), condition=%wide.region_11.12_spmd.clone, body=%wide.region_6.11_spmd.clone.sunk | while | flops 275976704 | bytes 9448853 | solution.py:139
  322.3 0.6 dynamic_slice.74
  323.6 0.7 slice.54
  325.7 0.6 dynamic_slice.74
  326.9 0.7 slice.54
  328.9 3.9 %conditional.3 = (f32[8,256]{1,0:T(8,128)S(1)}, f32[8,256]{1,0:T(8,128)S(1)}, f32[8,256,128]{2,1,0:T(8,128)S(1)}) conditional(s32[]{:T(128)} %convert_element_type.84, (s32[256]{0:T(256)S(1)}, s32[256]{0:T(256)S(1)}, s32[]{:T(128)}, s32[]{:T(128)}, bf16[8,256,128]{2,1,0:T(8,128)(2,1)}, /*index=5*/s32[]{:T(128)}, bf16[256,8,128]{2,0,1:T(8,128)(2,1)S(1)}, ...), branch_computations={%region_7.9_spmd, %region_10.10_spmd} | conditional | flops 275976704 | bytes 9429024 | solution.py:136
  329.1 1.3 fusion.2
  330.4 0.5 fusion.4
  330.9 1.9 convolution_add_fusion
  332.9 0.6 dynamic_slice.74
  334.1 0.7 slice.54
  336.1 3.9 %conditional.3 = (f32[8,256]{1,0:T(8,128)S(1)}, f32[8,256]{1,0:T(8,128)S(1)}, f32[8,256,128]{2,1,0:T(8,128)S(1)}) conditional(s32[]{:T(128)} %convert_element_type.84, (s32[256]{0:T(256)S(1)}, s32[256]{0:T(256)S(1)}, s32[]{:T(128)}, s32[]{:T(128)}, bf16[8,256,128]{2,1,0:T(8,128)(2,1)}, /*index=5*/s32[]{:T(128)}, bf16[256,8,128]{2,0,1:T(8,128)(2,1)S(1)}, ...), branch_computations={%region_7.9_spmd, %region_10.10_spmd} | conditional | flops 275976704 | bytes 9429024 | solution.py:136
  336.3 1.3 fusion.2
  337.6 0.5 fusion.4
  338.1 1.9 convolution_add_fusion
  340.1 0.6 dynamic_slice.74
  341.3 0.7 slice.54
  343.3 3.9 %conditional.3 = (f32[8,256]{1,0:T(8,128)S(1)}, f32[8,256]{1,0:T(8,128)S(1)}, f32[8,256,128]{2,1,0:T(8,128)S(1)}) conditional(s32[]{:T(128)} %convert_element_type.84, (s32[256]{0:T(256)S(1)}, s32[256]{0:T(256)S(1)}, s32[]{:T(128)}, s32[]{:T(128)}, bf16[8,256,128]{2,1,0:T(8,128)(2,1)}, /*index=5*/s32[]{:T(128)}, bf16[256,8,128]{2,0,1:T(8,128)(2,1)S(1)}, ...), branch_computations={%region_7.9_spmd, %region_10.10_spmd} | conditional | flops 275976704 | bytes 9429024 | solution.py:136
  343.5 1.3 fusion.2
  344.8 0.5 fusion.4
  345.3 1.9 convolution_add_fusion
  347.3 0.6 dynamic_slice.74
  348.5 0.7 slice.54
  350.5 3.9 %conditional.3 = (f32[8,256]{1,0:T(8,128)S(1)}, f32[8,256]{1,0:T(8,128)S(1)}, f32[8,256,128]{2,1,0:T(8,128)S(1)}) conditional(s32[]{:T(128)} %convert_element_type.84, (s32[256]{0:T(256)S(1)}, s32[256]{0:T(256)S(1)}, s32[]{:T(128)}, s32[]{:T(128)}, bf16[8,256,128]{2,1,0:T(8,128)(2,1)}, /*index=5*/s32[]{:T(128)}, bf16[256,8,128]{2,0,1:T(8,128)(2,1)S(1)}, ...), branch_computations={%region_7.9_spmd, %region_10.10_spmd} | conditional | flops 275976704 | bytes 9429024 | solution.py:136
  350.7 1.3 fusion.2
  352.0 0.5 fusion.4
  352.5 1.9 convolution_add_fusion
  354.5 0.6 dynamic_slice.74
  355.7 0.7 slice.54
  357.7 3.9 %conditional.3 = (f32[8,256]{1,0:T(8,128)S(1)}, f32[8,256]{1,0:T(8,128)S(1)}, f32[8,256,128]{2,1,0:T(8,128)S(1)}) conditional(s32[]{:T(128)} %convert_element_type.84, (s32[256]{0:T(256)S(1)}, s32[256]{0:T(256)S(1)}, s32[]{:T(128)}, s32[]{:T(128)}, bf16[8,256,128]{2,1,0:T(8,128)(2,1)}, /*index=5*/s32[]{:T(128)}, bf16[256,8,128]{2,0,1:T(8,128)(2,1)S(1)}, ...), branch_computations={%region_7.9_spmd, %region_10.10_spmd} | conditional | flops 275976704 | bytes 9429024 | solution.py:136
  357.9 1.3 fusion.2
  359.2 0.5 fusion.4
  359.8 1.9 convolution_add_fusion
  361.7 0.6 dynamic_slice.74
  362.9 0.7 slice.54
  365.0 0.6 dynamic_slice.74
  366.2 0.7 slice.54
  368.3 1.1 copy_bitcast_fusion
  369.6 0.8 reduce
  370.6 0.7 copy.51
  (97 shorter events, 4.9 us)
Async XLA Ops:
  7.2 19.4 %copy-start = (bf16[1024,512]{1,0:T(8,128)(2,1)S(1)}, bf16[1024,512]{1,0:T(8,128)(2,1)}, u32[]{:S(2)}) copy-start(bf16[1024,512]{1,0:T(8,128)(2,1)} %param.13) | copy-start | bytes 3145732
  7.2 44.7 %copy-start.2 = (bf16[1024,512]{1,0:T(8,128)(2,1)S(1)}, bf16[1024,512]{1,0:T(8,128)(2,1)}, u32[]{:S(2)}) copy-start(bf16[1024,512]{1,0:T(8,128)(2,1)} %param.12) | copy-start | bytes 3145732
  7.2 44.7 %all-gather.3.cloned.1.call-start = ((), (), s32[]{:S(2)}) async-start(), calls=%async_computation.2 | async-start | bytes 2621440 | tf_op jit(solution)/shard_map/all_gather | solution.py:65
  26.5 211.6 %reduce-scatter.2.cloned.1.call-start = ((), (), s32[]{:S(2)}) async-start(), calls=%async_computation.3 | async-start | bytes 11796480 | tf_op jit(solution)/shard_map/reduce_scatter | solution.py:67
  59.4 0.7 copy-start.3
  59.4 0.8 copy-start.1
  271.5 11.0 %slice-start = ((f32[256,1280]{0,1:T(8,128)}), f32[256,1024]{0,1:T(8,128)S(1)}, s32[]{:S(2)}) async-start(f32[256,1280]{0,1:T(8,128)} %reduce-scatter.2.cloned.1.call-done), calls=%async_computation.4 | async-start | bytes 2097152 | tf_op jit(solution)/shard_map/slice | solution.py:81
  274.8 94.7 %all-to-all-start = ((bf16[8,2,4096]{2,1,0:T(2,128)(2,1)}), bf16[8,2,4096]{2,1,0:T(2,128)(2,1)S(1)}, u32[]{:S(2)}, u32[]{:S(2)}) async-start(bf16[8,2,4096]{2,1,0:T(2,128)(2,1)} %reshape.274), calls=%async_computation.1 | async-start | bytes 262144 | tf_op jit(solution)/shard_map/all_to_all | solution.py:165
Sparse Core Ops, SparseCore 0:
  26.6 25.1 all-gather.2
  59.6 178.4 reduce-scatter.1
where the time goes:
time: 379 us; the launch traced here: 378 us
  waiting for transfers between devices  201 us (53%)
  blocking collectives  78.2 us (21%)
  matrix products  23.9 us (6%)
  local copies, waits for them, and re-layouts  23.1 us (6%)
  loops' own time  16.1 us (4%)
  between operations  14.3 us (4%)
  other arithmetic  13.8 us (4%)
  starting transfers between devices  7.88 us (2%)
    reduce_scatter x1, waiting for transfers between devices, local(): lax.psum_scatter(lax.dot_general(gathered, stacked, contract, preferred_e...  176 us
    all_gather x1, blocking collectives, local(): key_piece = lax.all_gather(keys, 'gy', axis=0, tiled=True)  32.4 us
    all_gather x1, blocking collectives, local(): value_piece = lax.all_gather(values, 'gy', axis=0, tiled=True)  30.6 us
    all_gather x1, waiting for transfers between devices, local(): gathered = lax.all_gather(normed, 'gx', axis=0, tiled=True)  25.2 us
    another operation x1, loops' own time, local(): lax.scan(one_block, initial, (key_blocks, value_blocks, offsets))  15.6 us
    psum x1, blocking collectives, local(): totals = lax.psum(squares, 'gy')  15.2 us
    dot_general x5, matrix products, compute(): jnp.einsum('hqk,kd->hqd', weights.astype(jnp.bfloat16), value_rows, prefe...  9.39 us
    unnamed x15, local copies, waits for them, and re-layouts  7.95 us
  transfers between devices with their start and end apart: 3, of which 2 were waited for; matrix products, arithmetic and copies ran while one was open for 11% of the time, Pallas kernels for 0%

commit v1 on v0

--- a/solution.py
+++ b/solution.py
@@ -3,7 +3,11 @@
 import jax
 import jax.numpy as jnp
 from jax import lax
+from jax.experimental import pallas as pl
+from jax.experimental.pallas import tpu as pltpu
 from jax.sharding import PartitionSpec as P
+
+MESH = pl.DeviceIdType.MESH
 
 D = 4096
 H = 32
@@ -179,9 +183,326 @@
     return (attention, cache_block)
 
 
+BLK = 256
+TWO_PI_PARTS = (6.28125, 4059.0 / 2**21, 2.0 * math.pi - 6.28125 - 4059.0 / 2**21)
+
+
+def fused_kernel(
+    lengths_ref, place_ref, hid_ref, gain_ref, freq_ref, wq_ref, wkv_ref,
+    out_ref, cache_ref,
+    squares, inverse, gain_other, x_own, x_other, w_other, normed, part, final,
+    up_out, up_in, down_out, down_in, kv_all, bias, cos_ref, sin_ref,
+    sq_send, sq_recv, inv_send, inv_recv, gain_sem, x_send, xo_recv, xn_recv,
+    w_send, w_recv, up_send, up_recv, down_send, down_recv, kz_send, ky_send, kv_recv,
+):
+    gx = lax.axis_index("gx")
+    gy = lax.axis_index("gy")
+    y = lax.rem(gy, 2)
+    z = lax.div(gy, 2)
+    core_peer = gx + 1 - 2 * lax.rem(gx, 2)
+    x_peer = lax.rem(gx + 2, 4)
+    far_peer = 3 - gx
+    y_peer = gy + 1 - 2 * y
+    depth = hid_ref.shape[1]
+    chunks = w_other.shape[0]
+
+    def remote(src, dst, send_sem, recv_sem, to_gx, to_gy):
+        return pltpu.make_async_remote_copy(
+            src_ref=src, dst_ref=dst, send_sem=send_sem, recv_sem=recv_sem,
+            device_id=(to_gx, to_gy), device_id_type=MESH,
+        )
+
+    barrier = pltpu.get_barrier_semaphore()
+    for step in range(1, 8):
+        pl.semaphore_signal(barrier, inc=1, device_id=(gx, lax.rem(gy + step, 8)), device_id_type=MESH)
+    for step in range(1, 4):
+        pl.semaphore_signal(barrier, inc=1, device_id=(lax.rem(gx + step, 4), gy), device_id_type=MESH)
+
+    widened = hid_ref[...].astype(jnp.float32)
+    squares[gy] = lax.dot_general(
+        jnp.ones((8, depth), jnp.float32), widened * widened, (((1,), (1,)), ((), ())),
+        precision=lax.Precision.HIGHEST, preferred_element_type=jnp.float32,
+    )
+    own_rows = pl.ds(pl.multiple_of(y * BLK, BLK), BLK)
+    other_rows = pl.ds(pl.multiple_of((1 - y) * BLK, BLK), BLK)
+    x_own[gx] = hid_ref[own_rows, :]
+    pl.semaphore_wait(barrier, 10)
+
+    sends = []
+
+    def go(copy):
+        copy.start()
+        sends.append(copy)
+
+    for step in range(1, 8):
+        go(remote(squares.at[gy], squares.at[gy], sq_send.at[step], sq_recv.at[gy], gx, lax.rem(gy + step, 8)))
+    go(remote(gain_ref, gain_other, gain_sem.at[0], gain_sem.at[1], gx, y_peer))
+    go(remote(hid_ref.at[other_rows, :], x_other.at[gx], x_send.at[0], xn_recv.at[gx], gx, y_peer))
+    go(remote(hid_ref.at[own_rows, :], x_own.at[gx], x_send.at[1], xo_recv.at[gx], x_peer, gy))
+    go(remote(hid_ref.at[own_rows, :], x_own.at[gx], x_send.at[2], xo_recv.at[gx], core_peer, gy))
+    kv_rows = pl.ds(pl.multiple_of(gx * 2 * HD, 2 * HD), 2 * HD)
+    go(remote(wkv_ref.at[kv_rows, :], w_other.at[0], w_send.at[0], w_recv.at[0], gx, y_peer))
+    for c in range(1, chunks):
+        go(remote(wq_ref.at[pl.ds((c - 1) * BLK, BLK), :], w_other.at[c], w_send.at[c], w_recv.at[c], gx, y_peer))
+
+    def arrived(dst, recv_sem):
+        remote(dst, dst, x_send.at[0], recv_sem, gx, y_peer).wait_recv()
+
+    first_token = gy * BLK
+    token = first_token + lax.broadcasted_iota(jnp.int32, (BLK, HD), 0)
+    opening = jnp.zeros((BLK, HD), jnp.int32)
+    end = jnp.zeros((1, HD), jnp.int32)
+    for s in range(lengths_ref.shape[0]):
+        end = end + lengths_ref[s : s + 1, :]
+        opening = jnp.where(token >= end, end, opening)
+    angles = (token - opening).astype(jnp.float32) * freq_ref[0:1, :]
+    turns = jnp.floor(angles * (0.5 / math.pi) + 0.5)
+    for piece in TWO_PI_PARTS:
+        angles = angles - turns * piece
+    cos_ref[...] = jnp.cos(angles)
+    sign = jnp.where(lax.broadcasted_iota(jnp.int32, (BLK, HD), 1) < HD // 2, -1.0, 1.0)
+    sin_ref[...] = jnp.sin(angles) * sign
+    window = bias.shape[1] // BLK
+    start_block = jnp.maximum(gy - (window - 1), 0)
+    for s in range(window):
+        for half in range(2):
+            lanes = s * BLK + half * HD
+            key = start_block * BLK + lanes + lax.broadcasted_iota(jnp.int32, (BLK, HD), 1)
+            bias[:, lanes : lanes + HD] = jnp.where((key >= opening) & (key <= token), 0.0, masked_out)
+
+    for step in range(1, 8):
+        source = lax.rem(gy + step, 8)
+        arrived(squares.at[source], sq_recv.at[source])
+    total = squares[0]
+    for s in range(1, 8):
+        total = total + squares[s]
+    inverse[gx] = lax.rsqrt(total / D + epsilon)
+    for step in range(1, 4):
+        go(remote(inverse.at[gx], inverse.at[gx], inv_send.at[step], inv_recv.at[gx], lax.rem(gx + step, 4), gy))
+
+    arrived(x_other.at[gx], xn_recv.at[gx])
+    go(remote(x_other.at[gx], x_other.at[gx], x_send.at[3], xn_recv.at[gx], x_peer, gy))
+    go(remote(x_other.at[gx], x_other.at[gx], x_send.at[4], xn_recv.at[gx], core_peer, gy))
+    arrived(x_own.at[x_peer], xo_recv.at[x_peer])
+    go(remote(x_own.at[x_peer], x_own.at[x_peer], x_send.at[5], xo_recv.at[x_peer], core_peer, gy))
+    arrived(x_other.at[x_peer], xn_recv.at[x_peer])
+    go(remote(x_other.at[x_peer], x_other.at[x_peer], x_send.at[6], xn_recv.at[x_peer], core_peer, gy))
+    arrived(gain_other, gain_sem.at[1])
+    for step in range(1, 4):
+        source = lax.rem(gx + step, 4)
+        arrived(inverse.at[source], inv_recv.at[source])
+    for peer in (core_peer, far_peer):
+        arrived(x_own.at[peer], xo_recv.at[peer])
+        arrived(x_other.at[peer], xn_recv.at[peer])
+
+    eighth = jnp.full((8, depth), 0.125, jnp.float32)
+
+    def normalise(m, carry):
+        scale = lax.dot_general(
+            inverse[m, :, own_rows], eighth, (((0,), (0,)), ((), ())),
+            precision=lax.Precision.HIGHEST, preferred_element_type=jnp.float32,
+        )
+        normed[m, :, 0:depth] = (x_own[m].astype(jnp.float32) * scale * gain_ref[0:1, :]).astype(jnp.bfloat16)
+        normed[m, :, depth:] = (x_other[m].astype(jnp.float32) * scale * gain_other[0:1, :]).astype(jnp.bfloat16)
+        return carry
+
+    lax.fori_loop(0, 4, normalise, 0)
+
+    contract = (((1,), (1,)), ((), ()))
+
+    def multiply(c, w_here):
+        arrived(w_other.at[c], w_recv.at[c])
+
+        def one(m, carry):
+            part[m] = lax.dot_general(
+                normed[m, :, 0:depth], w_here(), contract, preferred_element_type=jnp.float32
+            ) + lax.dot_general(
+                normed[m, :, depth:], w_other[c], contract, preferred_element_type=jnp.float32
+            )
+            return carry
+
+        lax.fori_loop(0, 4, one, 0)
+        final[c] = part[z]
+
+    def up_copy(c, t):
+        return remote(up_out.at[c, t], up_in.at[c, t], up_send.at[c, t], up_recv.at[c, t], gx, gy + 2)
+
+    def down_copy(c, t):
+        return remote(down_out.at[c, t], down_in.at[c, t], down_send.at[c, t], down_recv.at[c, t], gx, gy - 2)
+
+    def pass_on(c):
+        for t in (3, 2, 1):
+            @pl.when(z == 0)
+            def _():
+                up_out[c, t] = part[t].astype(jnp.bfloat16)
+                up_copy(c, t).start()
+
+            @pl.when((z > 0) & (z < t))
+            def _():
+                arrived(up_in.at[c, t], up_recv.at[c, t])
+                up_out[c, t] = (part[t] + up_in[c, t].astype(jnp.float32)).astype(jnp.bfloat16)
+                up_copy(c, t).start()
+
+            d = 3 - t
+
+            @pl.when(z == 3)
+            def _():
+                down_out[c, d] = part[d].astype(jnp.bfloat16)
+                down_copy(c, d).start()
+
+            @pl.when((z < 3) & (z > d))
+            def _():
+                arrived(down_in.at[c, d], down_recv.at[c, d])
+                down_out[c, d] = (part[d] + down_in[c, d].astype(jnp.float32)).astype(jnp.bfloat16)
+                down_copy(c, d).start()
+
+    def finish(c):
+        @pl.when(z > 0)
+        def _():
+            arrived(up_in.at[c, z], up_recv.at[c, z])
+            final[c] = final[c] + up_in[c, z].astype(jnp.float32)
+
+        @pl.when(z < 3)
+        def _():
+            arrived(down_in.at[c, z], down_recv.at[c, z])
+            final[c] = final[c] + down_in[c, z].astype(jnp.float32)
+
+    def rotated(u):
+        return (u * cos_ref[...] + pltpu.roll(u, HD // 2, 1) * sin_ref[...]).astype(jnp.bfloat16)
+
+    def q_chunk(c):
+        rows = pl.ds(pl.multiple_of((c - 1) * BLK, BLK), BLK)
+        multiply(c, lambda: wq_ref[rows, :])
+        pass_on(c)
+
+    multiply(0, lambda: wkv_ref[kv_rows, :])
+    pass_on(0)
+    q_chunk(1)
+
+    finish(0)
+    kv_all[gy, :, 0:HD] = rotated(final[0, :, 0:HD])
+    kv_all[gy, :, HD:] = final[0, :, HD:].astype(jnp.bfloat16)
+    for step in range(1, 4):
+        go(remote(kv_all.at[gy], kv_all.at[gy], kz_send.at[step], kv_recv.at[gy], gx, lax.rem(gy + 2 * step, 8)))
+    go(remote(kv_all.at[gy], kv_all.at[gy], ky_send.at[0], kv_recv.at[gy], gx, y_peer))
+    q_chunk(2)
+    for step in range(1, 4):
+        source = lax.rem(gy + 2 * step, 8)
+        arrived(kv_all.at[source], kv_recv.at[source])
+        go(remote(kv_all.at[source], kv_all.at[source], ky_send.at[step], kv_recv.at[source], gx, y_peer))
+
+    def late_chunk(c, carry):
+        q_chunk(c)
+        return carry
+
+    lax.fori_loop(3, chunks, late_chunk, 0)
+    for step in range(4):
+        source = lax.rem(y_peer + 2 * step, 8)
+        arrived(kv_all.at[source], kv_recv.at[source])
+
+    score_scale = 1.0 / math.sqrt(HD)
+    keys = pl.ds(start_block, window)
+
+    def attend(c, carry):
+        finish(c)
+        for half in range(2):
+            query = rotated(final[c, :, half * HD : (half + 1) * HD])
+            key_rows = kv_all[keys, :, 0:HD].reshape(window * BLK, HD)
+            value_rows = kv_all[keys, :, HD:].reshape(window * BLK, HD)
+            scores = lax.dot_general(query, key_rows, contract, preferred_element_type=jnp.float32)
+            scores = scores * score_scale + bias[...]
+            weights = jnp.exp(scores - jnp.max(scores, axis=1, keepdims=True))
+            sums = jnp.sum(weights, axis=1, keepdims=True)
+            mixed = jnp.dot(weights.astype(jnp.bfloat16), value_rows, preferred_element_type=jnp.float32)
+            column = pl.multiple_of((c - 1) * BLK + half * HD, HD)
+            out_ref[:, pl.ds(column, HD)] = (mixed / sums).astype(jnp.bfloat16)
+        return carry
+
+    lax.fori_loop(1, chunks, attend, 0)
+
+    wanted = gy * BLK + lax.broadcasted_iota(jnp.int32, (BLK, BLK), 0)
+    picked = jnp.zeros((BLK, 2 * HD), jnp.float32)
+    for s in range(8):
+        chosen = jnp.where(place_ref[:, s * BLK : (s + 1) * BLK] == wanted, 1.0, 0.0).astype(jnp.bfloat16)
+        picked = picked + jnp.dot(chosen, kv_all[s], preferred_element_type=jnp.float32)
+    cache_ref[...] = picked.astype(jnp.bfloat16).reshape(cache_ref.shape)
+
+    for copy in sends:
+        copy.wait_send()
+
+    def drain(c, carry):
+        for t in (3, 2, 1):
+            @pl.when(z < t)
+            def _():
+                up_copy(c, t).wait_send()
+
+            @pl.when(z > 3 - t)
+            def _():
+                down_copy(c, 3 - t).wait_send()
+        return carry
+
+    lax.fori_loop(0, chunks, drain, 0)
+
+
+def fused(hidden_in, norm_gain, query_proj, kv_proj, prompt_lengths, cache_slot):
+    width = hidden_in.shape[1]
+    query_cols = query_proj.shape[0]
+    chunks = 1 + query_cols // BLK
+    page_len = BLK // PAGES_DEV
+    places = (
+        cache_slot[:, None] * page_len + jnp.arange(page_len, dtype=jnp.int32)[None, :]
+    ).reshape(1, -1)
+    lengths = jnp.broadcast_to(prompt_lengths[:, None], (prompt_lengths.shape[0], HD))
+    gain = jnp.broadcast_to(norm_gain.astype(jnp.float32)[None, :], (8, width))
+    half_size = HD // 2
+    frequency = rope_base ** (-(jnp.arange(half_size, dtype=jnp.float32) * 2.0) / HD)
+    frequency = jnp.broadcast_to(jnp.concatenate([frequency, frequency])[None, :], (8, HD))
+    all_tokens = hidden_in.shape[0] * lax.axis_size("gx")
+    window = all_tokens // 2 // BLK + 1
+    bf16, f32 = jnp.bfloat16, jnp.float32
+    dma = pltpu.SemaphoreType.DMA
+    vmem = pl.BlockSpec(memory_space=pltpu.VMEM)
+    return pl.pallas_call(
+        fused_kernel,
+        out_shape=(
+            jax.ShapeDtypeStruct((BLK, query_cols), bf16),
+            jax.ShapeDtypeStruct((PAGES_DEV, page_len, 2 * HD), bf16),
+        ),
+        in_specs=[vmem] * 7,
+        out_specs=(vmem, vmem),
+        scratch_shapes=[
+            pltpu.VMEM((8, 8, 2 * BLK), f32),
+            pltpu.VMEM((4, 8, 2 * BLK), f32),
+            pltpu.VMEM((8, width), f32),
+            pltpu.VMEM((4, BLK, width), bf16),
+            pltpu.VMEM((4, BLK, width), bf16),
+            pltpu.VMEM((chunks, BLK, width), bf16),
+            pltpu.VMEM((4, BLK, 2 * width), bf16),
+            pltpu.VMEM((4, BLK, BLK), f32),
+            pltpu.VMEM((chunks, BLK, BLK), f32),
+            pltpu.VMEM((chunks, 4, BLK, BLK), bf16),
+            pltpu.VMEM((chunks, 4, BLK, BLK), bf16),
+            pltpu.VMEM((chunks, 4, BLK, BLK), bf16),
+            pltpu.VMEM((chunks, 4, BLK, BLK), bf16),
+            pltpu.VMEM((8, BLK, 2 * HD), bf16),
+            pltpu.VMEM((BLK, window * BLK), f32),
+            pltpu.VMEM((BLK, HD), f32),
+            pltpu.VMEM((BLK, HD), f32),
+            dma((8,)), dma((8,)), dma((4,)), dma((4,)), dma((2,)), dma((7,)), dma((4,)), dma((4,)),
+            dma((chunks,)), dma((chunks,)), dma((chunks, 4)), dma((chunks, 4)), dma((chunks, 4)), dma((chunks, 4)),
+            dma((4,)), dma((4,)), dma((8,)),
+        ],
+        compiler_params=pltpu.CompilerParams(
+            collective_id=0, has_side_effects=True, vmem_limit_bytes=56 * 1024 * 1024
+        ),
+        cost_estimate=pl.CostEstimate(flops=4000000000, bytes_accessed=8000000, transcendentals=3000000),
+    )(lengths, places, hidden_in, gain, frequency, query_proj, kv_proj)
+
+
 def solution(mesh):
+    form = fused if (mesh.shape["gx"], mesh.shape["gy"]) == (4, 8) else local
     return jax.shard_map(
-        local,
+        form,
         mesh=mesh,
         in_specs=(P("gx", "gy"), P("gy"), P("gx", "gy"), P(None, "gy"), P(), P()),
         out_specs=(P("gy", "gx"), P("gy", None, "gx")),

time: 379 us -> 111 us (0.29)
  the two profiles are of different devices: /device:TPU:22 before, /device:TPU:0 now
where the time goes in v1:
time: 111 us; the launch traced here: 109 us
  Pallas kernels  103 us (93%)
  local copies, waits for them, and re-layouts  5.2 us (5%)
    pallas_call x1, Pallas kernels, fused(): pl.pallas_call(fused_kernel, out_shape=(jax.ShapeDtypeStruct((BLK, query_...  103 us
    unnamed x8, local copies, waits for them, and re-layouts  2.64 us

profile of v1, /device:TPU:0, one launch (start us, length us, event | category | flops | bytes accessed | tf_op | source)
XLA Modules:
  0.0 109.3 jit_solution(12260363831295807775)
XLA Ops:
  0.6 0.7 broadcast_multiply_fusion
  1.3 0.1 pad_maximum_fusion
  1.4 0.0 copy-start.2
  1.4 0.6 broadcast_in_dim.8.freq_ref
  2.0 0.1 copy-done.2
  2.0 0.0 copy-start.1
  2.0 0.7 broadcast_in_dim.6.lengths_ref
  2.7 0.0 copy-done.1
  2.7 0.6 broadcast_in_dim.7.gain_ref
  3.3 0.1 iota_add_fusion
  3.4 0.7 add.26.place_ref
  4.1 102.6 %shard_map.77 = (bf16[256,1024]{1,0:T(8,128)(2,1)}, bf16[16,16,256]{2,1,0:T(8,128)(2,1)}) custom-call(s32[8,128]{1,0:T(8,128)} %broadcast_in_dim.6.lengths_ref, s32[1,2048]{1,0:T(1,128)} %add.26.place_ref, bf16[512,512]{1,0:T(8,128)(2,1)} %hid_ref.1, f32[8,512]{1,0:T(8,128)} %broadcast_in_dim.7.gain_ref, f32[8,128]{1,0:T(8,128)} %broadcast_in_dim.8.freq_ref, ...), custom_call_target="tpu_custom_call" | custom-call | flops 4000000000 | bytes 8000000 | tf_op jit(solution)/shard_map/pallas_call | solution.py:465
  106.8 0.0 copy-start
  106.8 1.9 %copy.10 = bf16[256,1024]{1,0:T(8,128)(2,1)} copy(bf16[256,1024]{1,0:T(8,128)(2,1)} %get-tuple-element.4) | data formatting | bytes 1048576
  108.7 0.0 copy-done
  108.7 0.7 copy.11
  (1 shorter events, 0.0 us)
Async XLA Ops:
  1.4 0.7 copy-start.2
  2.0 0.7 copy-start.1
  106.8 1.9 %copy-start = (bf16[16,16,256]{2,1,0:T(8,128)(2,1)S(1)}, bf16[16,16,256]{2,1,0:T(8,128)(2,1)}, u32[]{:S(2)}) copy-start(bf16[16,16,256]{2,1,0:T(8,128)(2,1)} %get-tuple-element.5) | copy-start | bytes 393220

commit v2 on v1

--- a/solution.py
+++ b/solution.py
@@ -2,6 +2,7 @@
 
 import jax
 import jax.numpy as jnp
+import numpy as np
 from jax import lax
 from jax.experimental import pallas as pl
 from jax.experimental.pallas import tpu as pltpu
@@ -188,9 +189,9 @@
 
 
 def fused_kernel(
-    lengths_ref, place_ref, hid_ref, gain_ref, freq_ref, wq_ref, wkv_ref,
+    lengths_ref, slot_ref, hid_ref, gain_row, freq_ref, wq_ref, wkv_ref,
     out_ref, cache_ref,
-    squares, inverse, gain_other, x_own, x_other, w_other, normed, part, final,
+    squares, inverse, gain_ref, gain_other, x_own, x_other, w_other, normed, part, final,
     up_out, up_in, down_out, down_in, kv_all, bias, cos_ref, sin_ref,
     sq_send, sq_recv, inv_send, inv_recv, gain_sem, x_send, xo_recv, xn_recv,
     w_send, w_recv, up_send, up_recv, down_send, down_recv, kz_send, ky_send, kv_recv,
@@ -226,6 +227,7 @@
     own_rows = pl.ds(pl.multiple_of(y * BLK, BLK), BLK)
     other_rows = pl.ds(pl.multiple_of((1 - y) * BLK, BLK), BLK)
     x_own[gx] = hid_ref[own_rows, :]
+    gain_ref[...] = jnp.broadcast_to(gain_row[...].astype(jnp.float32), gain_ref.shape)
     pl.semaphore_wait(barrier, 10)
 
     sends = []
@@ -241,9 +243,10 @@
     go(remote(hid_ref.at[own_rows, :], x_own.at[gx], x_send.at[1], xo_recv.at[gx], x_peer, gy))
     go(remote(hid_ref.at[own_rows, :], x_own.at[gx], x_send.at[2], xo_recv.at[gx], core_peer, gy))
     kv_rows = pl.ds(pl.multiple_of(gx * 2 * HD, 2 * HD), 2 * HD)
-    go(remote(wkv_ref.at[kv_rows, :], w_other.at[0], w_send.at[0], w_recv.at[0], gx, y_peer))
-    for c in range(1, chunks):
-        go(remote(wq_ref.at[pl.ds((c - 1) * BLK, BLK), :], w_other.at[c], w_send.at[c], w_recv.at[c], gx, y_peer))
+
+    def send_weights(c):
+        rows = wkv_ref.at[kv_rows, :] if c == 0 else wq_ref.at[pl.ds((c - 1) * BLK, BLK), :]
+        go(remote(rows, w_other.at[c], w_send.at[c], w_recv.at[c], gx, y_peer))
 
     def arrived(dst, recv_sem):
         remote(dst, dst, x_send.at[0], recv_sem, gx, y_peer).wait_recv()
@@ -252,8 +255,8 @@
     token = first_token + lax.broadcasted_iota(jnp.int32, (BLK, HD), 0)
     opening = jnp.zeros((BLK, HD), jnp.int32)
     end = jnp.zeros((1, HD), jnp.int32)
-    for s in range(lengths_ref.shape[0]):
-        end = end + lengths_ref[s : s + 1, :]
+    for s in range(lengths_ref.shape[1]):
+        end = end + lengths_ref[0:1, s : s + 1]
         opening = jnp.where(token >= end, end, opening)
     angles = (token - opening).astype(jnp.float32) * freq_ref[0:1, :]
     turns = jnp.floor(angles * (0.5 / math.pi) + 0.5)
@@ -280,38 +283,44 @@
     for step in range(1, 4):
         go(remote(inverse.at[gx], inverse.at[gx], inv_send.at[step], inv_recv.at[gx], lax.rem(gx + step, 4), gy))
 
-    arrived(x_other.at[gx], xn_recv.at[gx])
-    go(remote(x_other.at[gx], x_other.at[gx], x_send.at[3], xn_recv.at[gx], x_peer, gy))
-    go(remote(x_other.at[gx], x_other.at[gx], x_send.at[4], xn_recv.at[gx], core_peer, gy))
-    arrived(x_own.at[x_peer], xo_recv.at[x_peer])
-    go(remote(x_own.at[x_peer], x_own.at[x_peer], x_send.at[5], xo_recv.at[x_peer], core_peer, gy))
-    arrived(x_other.at[x_peer], xn_recv.at[x_peer])
-    go(remote(x_other.at[x_peer], x_other.at[x_peer], x_send.at[6], xn_recv.at[x_peer], core_peer, gy))
-    arrived(gain_other, gain_sem.at[1])
-    for step in range(1, 4):
-        source = lax.rem(gx + step, 4)
-        arrived(inverse.at[source], inv_recv.at[source])
-    for peer in (core_peer, far_peer):
-        arrived(x_own.at[peer], xo_recv.at[peer])
-        arrived(x_other.at[peer], xn_recv.at[peer])
-
     eighth = jnp.full((8, depth), 0.125, jnp.float32)
 
-    def normalise(m, carry):
+    def normalise(m):
         scale = lax.dot_general(
             inverse[m, :, own_rows], eighth, (((0,), (0,)), ((), ())),
             precision=lax.Precision.HIGHEST, preferred_element_type=jnp.float32,
         )
         normed[m, :, 0:depth] = (x_own[m].astype(jnp.float32) * scale * gain_ref[0:1, :]).astype(jnp.bfloat16)
         normed[m, :, depth:] = (x_other[m].astype(jnp.float32) * scale * gain_other[0:1, :]).astype(jnp.bfloat16)
-        return carry
-
-    lax.fori_loop(0, 4, normalise, 0)
+
+    arrived(x_other.at[gx], xn_recv.at[gx])
+    go(remote(x_other.at[gx], x_other.at[gx], x_send.at[3], xn_recv.at[gx], x_peer, gy))
+    go(remote(x_other.at[gx], x_other.at[gx], x_send.at[4], xn_recv.at[gx], core_peer, gy))
+    send_weights(0)
+    arrived(x_own.at[x_peer], xo_recv.at[x_peer])
+    go(remote(x_own.at[x_peer], x_own.at[x_peer], x_send.at[5], xo_recv.at[x_peer], core_peer, gy))
+    arrived(gain_other, gain_sem.at[1])
+    normalise(gx)
+    arrived(x_own.at[core_peer], xo_recv.at[core_peer])
+    arrived(x_other.at[core_peer], xn_recv.at[core_peer])
+    arrived(inverse.at[core_peer], inv_recv.at[core_peer])
+    normalise(core_peer)
+    arrived(x_other.at[x_peer], xn_recv.at[x_peer])
+    go(remote(x_other.at[x_peer], x_other.at[x_peer], x_send.at[6], xn_recv.at[x_peer], core_peer, gy))
+    send_weights(1)
+    arrived(inverse.at[x_peer], inv_recv.at[x_peer])
+    normalise(x_peer)
+    arrived(inverse.at[far_peer], inv_recv.at[far_peer])
+    arrived(x_own.at[far_peer], xo_recv.at[far_peer])
+    arrived(x_other.at[far_peer], xn_recv.at[far_peer])
+    normalise(far_peer)
 
     contract = (((1,), (1,)), ((), ()))
 
     def multiply(c, w_here):
         arrived(w_other.at[c], w_recv.at[c])
+        if isinstance(c, int) and c + 2 < chunks:
+            send_weights(c + 2)
 
         def one(m, carry):
             part[m] = lax.dot_general(
@@ -330,10 +339,14 @@
     def down_copy(c, t):
         return remote(down_out.at[c, t], down_in.at[c, t], down_send.at[c, t], down_recv.at[c, t], gx, gy - 2)
 
-    def pass_on(c):
+    def pass_on(c, first=False):
         for t in (3, 2, 1):
             @pl.when(z == 0)
             def _():
+                if t == 1:
+                    up_copy(c, 3).wait_send()
+                elif not first:
+                    up_copy(c - 1, t - 1).wait_send()
                 up_out[c, t] = part[t].astype(jnp.bfloat16)
                 up_copy(c, t).start()
 
@@ -347,6 +360,10 @@
 
             @pl.when(z == 3)
             def _():
+                if t == 1:
+                    down_copy(c, 0).wait_send()
+                elif not first:
+                    down_copy(c - 1, d + 1).wait_send()
                 down_out[c, d] = part[d].astype(jnp.bfloat16)
                 down_copy(c, d).start()
 
@@ -376,26 +393,62 @@
         pass_on(c)
 
     multiply(0, lambda: wkv_ref[kv_rows, :])
-    pass_on(0)
+    pass_on(0, True)
     q_chunk(1)
 
     finish(0)
     kv_all[gy, :, 0:HD] = rotated(final[0, :, 0:HD])
     kv_all[gy, :, HD:] = final[0, :, HD:].astype(jnp.bfloat16)
-    for step in range(1, 4):
-        go(remote(kv_all.at[gy], kv_all.at[gy], kz_send.at[step], kv_recv.at[gy], gx, lax.rem(gy + 2 * step, 8)))
-    go(remote(kv_all.at[gy], kv_all.at[gy], ky_send.at[0], kv_recv.at[gy], gx, y_peer))
+
+    def kv_up(step):
+        block = kv_all.at[gy - 2 * step]
+        return remote(block, block, kz_send.at[0, step], kv_recv.at[gy - 2 * step], gx, gy + 2)
+
+    def kv_down(step):
+        block = kv_all.at[gy + 2 * step]
+        return remote(block, block, kz_send.at[1, step], kv_recv.at[gy + 2 * step], gx, gy - 2)
+
+    def kv_across(source, side, step):
+        return remote(kv_all.at[source], kv_all.at[source], ky_send.at[side, step], kv_recv.at[source], gx, y_peer)
+
+    def kv_step(step, act):
+        @pl.when((z >= step) & (z < 3))
+        def _():
+            act(kv_up(step))
+
+        @pl.when((z + step <= 3) & (z > 0))
+        def _():
+            act(kv_down(step))
+
+        if step == 0:
+            act(kv_across(gy, 0, 0))
+        else:
+            @pl.when(z >= step)
+            def _():
+                act(kv_across(gy - 2 * step, 0, step))
+
+            @pl.when(z + step <= 3)
+            def _():
+                act(kv_across(gy + 2 * step, 1, step))
+
+    def kv_forward(step):
+        @pl.when(z >= step)
+        def _():
+            arrived(kv_all.at[gy - 2 * step], kv_recv.at[gy - 2 * step])
+
+        @pl.when(z + step <= 3)
+        def _():
+            arrived(kv_all.at[gy + 2 * step], kv_recv.at[gy + 2 * step])
+
+        kv_step(step, lambda copy: copy.start())
+
+    kv_step(0, lambda copy: copy.start())
     q_chunk(2)
-    for step in range(1, 4):
-        source = lax.rem(gy + 2 * step, 8)
-        arrived(kv_all.at[source], kv_recv.at[source])
-        go(remote(kv_all.at[source], kv_all.at[source], ky_send.at[step], kv_recv.at[source], gx, y_peer))
-
-    def late_chunk(c, carry):
-        q_chunk(c)
-        return carry
-
-    lax.fori_loop(3, chunks, late_chunk, 0)
+    kv_forward(1)
+    q_chunk(3)
+    kv_forward(2)
+    q_chunk(4)
+    kv_forward(3)
     for step in range(4):
         source = lax.rem(y_peer + 2 * step, 8)
         arrived(kv_all.at[source], kv_recv.at[source])
@@ -420,43 +473,59 @@
 
     lax.fori_loop(1, chunks, attend, 0)
 
-    wanted = gy * BLK + lax.broadcasted_iota(jnp.int32, (BLK, BLK), 0)
+    page_len = cache_ref.shape[1]
+    pages = slot_ref.shape[1]
+    wanted = (gy * BLK + lax.broadcasted_iota(jnp.int32, (BLK, BLK), 0)).astype(jnp.float32)
+    page = lax.broadcasted_iota(jnp.int32, (pages, BLK), 0)
+    lane = lax.broadcasted_iota(jnp.int32, (pages, BLK), 1)
+    offset = lax.rem(lane[0:8, :], page_len).astype(jnp.float32)
+    slots = jnp.broadcast_to(slot_ref[...].astype(jnp.float32), (8, pages)).astype(jnp.bfloat16)
     picked = jnp.zeros((BLK, 2 * HD), jnp.float32)
     for s in range(8):
-        chosen = jnp.where(place_ref[:, s * BLK : (s + 1) * BLK] == wanted, 1.0, 0.0).astype(jnp.bfloat16)
+        spread = jnp.where(page == s * PAGES_DEV + lax.div(lane, page_len), 1.0, 0.0).astype(jnp.bfloat16)
+        places = jnp.dot(slots, spread, preferred_element_type=jnp.float32) * page_len + offset
+        chosen = jnp.where(places[0:1, :] == wanted, 1.0, 0.0).astype(jnp.bfloat16)
         picked = picked + jnp.dot(chosen, kv_all[s], preferred_element_type=jnp.float32)
     cache_ref[...] = picked.astype(jnp.bfloat16).reshape(cache_ref.shape)
 
     for copy in sends:
         copy.wait_send()
 
+    for step in range(4):
+        kv_step(step, lambda copy: copy.wait_send())
+
     def drain(c, carry):
-        for t in (3, 2, 1):
-            @pl.when(z < t)
+        for t in (3, 2):
+            @pl.when((z > 0) & (z < t))
             def _():
                 up_copy(c, t).wait_send()
 
-            @pl.when(z > 3 - t)
+            @pl.when((z < 3) & (z > 3 - t))
             def _():
                 down_copy(c, 3 - t).wait_send()
         return carry
 
     lax.fori_loop(0, chunks, drain, 0)
+
+    @pl.when(z == 0)
+    def _():
+        up_copy(chunks - 1, 2).wait_send()
+        up_copy(chunks - 1, 1).wait_send()
+
+    @pl.when(z == 3)
+    def _():
+        down_copy(chunks - 1, 1).wait_send()
+        down_copy(chunks - 1, 2).wait_send()
 
 
 def fused(hidden_in, norm_gain, query_proj, kv_proj, prompt_lengths, cache_slot):
     width = hidden_in.shape[1]
     query_cols = query_proj.shape[0]
     chunks = 1 + query_cols // BLK
+    exponents = np.arange(HD // 2, dtype=np.float32) * 2.0 / HD
+    frequency = np.float32(rope_base) ** -np.concatenate([exponents, exponents]).astype(np.float32)
+    frequency = jnp.asarray(frequency[None, :])
     page_len = BLK // PAGES_DEV
-    places = (
-        cache_slot[:, None] * page_len + jnp.arange(page_len, dtype=jnp.int32)[None, :]
-    ).reshape(1, -1)
-    lengths = jnp.broadcast_to(prompt_lengths[:, None], (prompt_lengths.shape[0], HD))
-    gain = jnp.broadcast_to(norm_gain.astype(jnp.float32)[None, :], (8, width))
-    half_size = HD // 2
-    frequency = rope_base ** (-(jnp.arange(half_size, dtype=jnp.float32) * 2.0) / HD)
-    frequency = jnp.broadcast_to(jnp.concatenate([frequency, frequency])[None, :], (8, HD))
     all_tokens = hidden_in.shape[0] * lax.axis_size("gx")
     window = all_tokens // 2 // BLK + 1
     bf16, f32 = jnp.bfloat16, jnp.float32
@@ -474,6 +543,7 @@
             pltpu.VMEM((8, 8, 2 * BLK), f32),
             pltpu.VMEM((4, 8, 2 * BLK), f32),
             pltpu.VMEM((8, width), f32),
+            pltpu.VMEM((8, width), f32),
             pltpu.VMEM((4, BLK, width), bf16),
             pltpu.VMEM((4, BLK, width), bf16),
             pltpu.VMEM((chunks, BLK, width), bf16),
@@ -490,13 +560,15 @@
             pltpu.VMEM((BLK, HD), f32),
             dma((8,)), dma((8,)), dma((4,)), dma((4,)), dma((2,)), dma((7,)), dma((4,)), dma((4,)),
             dma((chunks,)), dma((chunks,)), dma((chunks, 4)), dma((chunks, 4)), dma((chunks, 4)), dma((chunks, 4)),
-            dma((4,)), dma((4,)), dma((8,)),
+            dma((2, 4)), dma((2, 4)), dma((8,)),
         ],
         compiler_params=pltpu.CompilerParams(
             collective_id=0, has_side_effects=True, vmem_limit_bytes=56 * 1024 * 1024
         ),
         cost_estimate=pl.CostEstimate(flops=4000000000, bytes_accessed=8000000, transcendentals=3000000),
-    )(lengths, places, hidden_in, gain, frequency, query_proj, kv_proj)
+    )(
+        prompt_lengths[None, :], cache_slot[None, :], hidden_in, norm_gain[None, :], frequency, query_proj, kv_proj
+    )
 
 
 def solution(mesh):

time: 111 us -> 100 us (0.901); the launches traced: 109 us -> 100 us
  Pallas kernels: 103 us -> 95.5 us
  local copies, waits for them, and re-layouts: 5.2 us -> 3.82 us
    pallas_call x1, Pallas kernels: 103 us -> 95.5 us  [fused(): pl.pallas_call(fused_kernel, out_shape=(jax.ShapeDtypeStruct((BLK, query_...]
    broadcast_in_dim x3 -> x1, local copies, waits for them, and re-layouts: 1.87 us -> 0.58 us  [fused(): norm_gain[None, :]]
    unnamed x8 -> x6, local copies, waits for them, and re-layouts: 2.64 us -> 3.24 us
where the time goes in v2:
time: 100 us
  Pallas kernels  95.5 us (96%)
  local copies, waits for them, and re-layouts  3.82 us (4%)
    pallas_call x1, Pallas kernels, fused(): pl.pallas_call(fused_kernel, out_shape=(jax.ShapeDtypeStruct((BLK, query_...  95.5 us
    unnamed x6, local copies, waits for them, and re-layouts  3.24 us

profile of v2, /device:TPU:0, one launch (start us, length us, event | category | flops | bytes accessed | tf_op | source)
XLA Modules:
  0.0 100.0 jit_solution(8851447632759978550)
XLA Ops:
  0.6 0.0 copy-start.1
  0.6 0.7 copy-done.1
  1.3 0.6 broadcast_in_dim.11.gain_row
  1.9 95.5 %shard_map.86 = (bf16[256,1024]{1,0:T(8,128)(2,1)}, bf16[16,16,256]{2,1,0:T(8,128)(2,1)}) custom-call(s32[1,8]{1,0:T(1,128)} %bitcast.2, s32[1,128]{1,0:T(1,128)} %bitcast.3, bf16[512,512]{1,0:T(8,128)(2,1)} %hid_ref.1, bf16[1,512]{1,0:T(2,128)(2,1)} %broadcast_in_dim.11.gain_row, f32[1,128]{1,0:T(1,128)} %constant.2.clone.freq_ref, ...), custom_call_target="tpu_custom_call" | custom-call | flops 4000000000 | bytes 8000000 | tf_op jit(solution)/shard_map/pallas_call | solution.py:534
  97.4 0.0 copy-start
  97.4 1.9 %copy.11 = bf16[256,1024]{1,0:T(8,128)(2,1)} copy(bf16[256,1024]{1,0:T(8,128)(2,1)} %get-tuple-element.4) | data formatting | bytes 1048576
  99.3 0.0 copy-done
  99.3 0.7 copy.12
Async XLA Ops:
  0.6 0.7 copy-start.1
  97.4 1.9 %copy-start = (bf16[16,16,256]{2,1,0:T(8,128)(2,1)S(1)}, bf16[16,16,256]{2,1,0:T(8,128)(2,1)}, u32[]{:S(2)}) copy-start(bf16[16,16,256]{2,1,0:T(8,128)(2,1)} %get-tuple-element.5) | copy-start | bytes 393220

commit v3 on v2

--- a/solution.py
+++ b/solution.py
@@ -333,19 +333,22 @@
         lax.fori_loop(0, 4, one, 0)
         final[c] = part[z]
 
+    def start_of_chain(c):
+        return isinstance(c, int) and c == 0
+
     def up_copy(c, t):
         return remote(up_out.at[c, t], up_in.at[c, t], up_send.at[c, t], up_recv.at[c, t], gx, gy + 2)
 
     def down_copy(c, t):
         return remote(down_out.at[c, t], down_in.at[c, t], down_send.at[c, t], down_recv.at[c, t], gx, gy - 2)
 
-    def pass_on(c, first=False):
+    def pass_on(c, beside=None):
         for t in (3, 2, 1):
             @pl.when(z == 0)
             def _():
                 if t == 1:
                     up_copy(c, 3).wait_send()
-                elif not first:
+                elif not start_of_chain(c):
                     up_copy(c - 1, t - 1).wait_send()
                 up_out[c, t] = part[t].astype(jnp.bfloat16)
                 up_copy(c, t).start()
@@ -362,7 +365,7 @@
             def _():
                 if t == 1:
                     down_copy(c, 0).wait_send()
-                elif not first:
+                elif not start_of_chain(c):
                     down_copy(c - 1, d + 1).wait_send()
                 down_out[c, d] = part[d].astype(jnp.bfloat16)
                 down_copy(c, d).start()
@@ -373,6 +376,9 @@
                 down_out[c, d] = (part[d] + down_in[c, d].astype(jnp.float32)).astype(jnp.bfloat16)
                 down_copy(c, d).start()
 
+            if beside is not None:
+                beside(3 - t)
+
     def finish(c):
         @pl.when(z > 0)
         def _():
@@ -387,18 +393,10 @@
     def rotated(u):
         return (u * cos_ref[...] + pltpu.roll(u, HD // 2, 1) * sin_ref[...]).astype(jnp.bfloat16)
 
-    def q_chunk(c):
+    def q_chunk(c, beside):
         rows = pl.ds(pl.multiple_of((c - 1) * BLK, BLK), BLK)
         multiply(c, lambda: wq_ref[rows, :])
-        pass_on(c)
-
-    multiply(0, lambda: wkv_ref[kv_rows, :])
-    pass_on(0, True)
-    q_chunk(1)
-
-    finish(0)
-    kv_all[gy, :, 0:HD] = rotated(final[0, :, 0:HD])
-    kv_all[gy, :, HD:] = final[0, :, HD:].astype(jnp.bfloat16)
+        pass_on(c, beside)
 
     def kv_up(step):
         block = kv_all.at[gy - 2 * step]
@@ -442,36 +440,49 @@
 
         kv_step(step, lambda copy: copy.start())
 
-    kv_step(0, lambda copy: copy.start())
-    q_chunk(2)
-    kv_forward(1)
-    q_chunk(3)
-    kv_forward(2)
-    q_chunk(4)
-    kv_forward(3)
+    score_scale = math.log2(math.e) / math.sqrt(HD)
+    keys = pl.ds(start_block, window)
+
+    def attend(head):
+        c = 1 + lax.div(head, 2)
+
+        @pl.when(lax.rem(head, 2) == 0)
+        def _():
+            finish(c)
+
+        lanes = pl.ds(pl.multiple_of(lax.rem(head, 2) * HD, HD), HD)
+        query = rotated(final[c, :, lanes])
+        key_rows = kv_all[keys, :, 0:HD].reshape(window * BLK, HD)
+        value_rows = kv_all[keys, :, HD:].reshape(window * BLK, HD)
+        scores = lax.dot_general(query, key_rows, contract, preferred_element_type=jnp.float32)
+        scores = scores * score_scale + bias[...]
+        weights = jnp.exp2(scores - jnp.max(scores, axis=1, keepdims=True))
+        sums = jnp.sum(weights, axis=1, keepdims=True)
+        mixed = jnp.dot(weights.astype(jnp.bfloat16), value_rows, preferred_element_type=jnp.float32)
+        out_ref[:, pl.ds(pl.multiple_of(head * HD, HD), HD)] = (mixed / sums).astype(jnp.bfloat16)
+
+    def share_kv(step):
+        if step == 1:
+            finish(0)
+            kv_all[gy, :, 0:HD] = rotated(final[0, :, 0:HD])
+            kv_all[gy, :, HD:] = final[0, :, HD:].astype(jnp.bfloat16)
+            kv_step(0, lambda copy: copy.start())
+
+    multiply(0, lambda: wkv_ref[kv_rows, :])
+    pass_on(0)
+    q_chunk(1, share_kv)
+    q_chunk(2, lambda step: kv_forward(step + 1))
     for step in range(4):
         source = lax.rem(y_peer + 2 * step, 8)
         arrived(kv_all.at[source], kv_recv.at[source])
 
-    score_scale = 1.0 / math.sqrt(HD)
-    keys = pl.ds(start_block, window)
-
-    def attend(c, carry):
-        finish(c)
-        for half in range(2):
-            query = rotated(final[c, :, half * HD : (half + 1) * HD])
-            key_rows = kv_all[keys, :, 0:HD].reshape(window * BLK, HD)
-            value_rows = kv_all[keys, :, HD:].reshape(window * BLK, HD)
-            scores = lax.dot_general(query, key_rows, contract, preferred_element_type=jnp.float32)
-            scores = scores * score_scale + bias[...]
-            weights = jnp.exp(scores - jnp.max(scores, axis=1, keepdims=True))
-            sums = jnp.sum(weights, axis=1, keepdims=True)
-            mixed = jnp.dot(weights.astype(jnp.bfloat16), value_rows, preferred_element_type=jnp.float32)
-            column = pl.multiple_of((c - 1) * BLK + half * HD, HD)
-            out_ref[:, pl.ds(column, HD)] = (mixed / sums).astype(jnp.bfloat16)
+    early = 3 * (chunks - 3)
+
+    def late_chunk(c, carry):
+        q_chunk(c, lambda step: attend((c - 3) * 3 + step))
         return carry
 
-    lax.fori_loop(1, chunks, attend, 0)
+    lax.fori_loop(3, chunks, late_chunk, 0)
 
     page_len = cache_ref.shape[1]
     pages = slot_ref.shape[1]
@@ -487,6 +498,12 @@
         chosen = jnp.where(places[0:1, :] == wanted, 1.0, 0.0).astype(jnp.bfloat16)
         picked = picked + jnp.dot(chosen, kv_all[s], preferred_element_type=jnp.float32)
     cache_ref[...] = picked.astype(jnp.bfloat16).reshape(cache_ref.shape)
+
+    def late_head(head, carry):
+        attend(head)
+        return carry
+
+    lax.fori_loop(early, 2 * (chunks - 1), late_head, 0)
 
     for copy in sends:
         copy.wait_send()

time: 100 us -> 117 us (1.17)
  Pallas kernels: 95.5 us -> 112 us
    pallas_call x1, Pallas kernels: 95.5 us -> 112 us  [fused(): pl.pallas_call(fused_kernel, out_shape=(jax.ShapeDtypeStruct((BLK, query_...]
where the time goes in v3:
time: 117 us
  Pallas kernels  112 us (96%)
  local copies, waits for them, and re-layouts  3.82 us (3%)
    pallas_call x1, Pallas kernels, fused(): pl.pallas_call(fused_kernel, out_shape=(jax.ShapeDtypeStruct((BLK, query_...  112 us
    unnamed x6, local copies, waits for them, and re-layouts  3.24 us

profile of v3, /device:TPU:0, one launch (start us, length us, event | category | flops | bytes accessed | tf_op | source)
XLA Modules:
  0.0 116.8 jit_solution(11516370979833309)
XLA Ops:
  0.6 0.0 copy-start.1
  0.6 0.7 copy-done.1
  1.3 0.6 broadcast_in_dim.11.gain_row
  1.9 112.3 %shard_map.86 = (bf16[256,1024]{1,0:T(8,128)(2,1)}, bf16[16,16,256]{2,1,0:T(8,128)(2,1)}) custom-call(s32[1,8]{1,0:T(1,128)} %bitcast.2, s32[1,128]{1,0:T(1,128)} %bitcast.3, bf16[512,512]{1,0:T(8,128)(2,1)} %hid_ref.1, bf16[1,512]{1,0:T(2,128)(2,1)} %broadcast_in_dim.11.gain_row, f32[1,128]{1,0:T(1,128)} %constant.2.clone.freq_ref, ...), custom_call_target="tpu_custom_call" | custom-call | flops 4000000000 | bytes 8000000 | tf_op jit(solution)/shard_map/pallas_call | solution.py:551
  114.2 0.0 copy-start
  114.2 1.9 %copy.11 = bf16[256,1024]{1,0:T(8,128)(2,1)} copy(bf16[256,1024]{1,0:T(8,128)(2,1)} %get-tuple-element.4) | data formatting | bytes 1048576
  116.1 0.0 copy-done
  116.1 0.7 copy.12
Async XLA Ops:
  0.6 0.7 copy-start.1
  114.2 1.9 %copy-start = (bf16[16,16,256]{2,1,0:T(8,128)(2,1)S(1)}, bf16[16,16,256]{2,1,0:T(8,128)(2,1)}, u32[]{:S(2)}) copy-start(bf16[16,16,256]{2,1,0:T(8,128)(2,1)} %get-tuple-element.5) | copy-start | bytes 393220

commit v4 on v3

--- a/solution.py
+++ b/solution.py
@@ -323,7 +323,7 @@
             send_weights(c + 2)
 
         def one(m, carry):
-            part[m] = lax.dot_general(
+            part[c % 2, m] = lax.dot_general(
                 normed[m, :, 0:depth], w_here(), contract, preferred_element_type=jnp.float32
             ) + lax.dot_general(
                 normed[m, :, depth:], w_other[c], contract, preferred_element_type=jnp.float32
@@ -331,10 +331,7 @@
             return carry
 
         lax.fori_loop(0, 4, one, 0)
-        final[c] = part[z]
-
-    def start_of_chain(c):
-        return isinstance(c, int) and c == 0
+        final[c] = part[c % 2, z]
 
     def up_copy(c, t):
         return remote(up_out.at[c, t], up_in.at[c, t], up_send.at[c, t], up_recv.at[c, t], gx, gy + 2)
@@ -342,42 +339,60 @@
     def down_copy(c, t):
         return remote(down_out.at[c, t], down_in.at[c, t], down_send.at[c, t], down_recv.at[c, t], gx, gy - 2)
 
+    def forward_up(c, t):
+        arrived(up_in.at[c, t], up_recv.at[c, t])
+        up_out[c, t] = (part[c % 2, t] + up_in[c, t].astype(jnp.float32)).astype(jnp.bfloat16)
+        up_copy(c, t).start()
+
+    def forward_down(c, d):
+        arrived(down_in.at[c, d], down_recv.at[c, d])
+        down_out[c, d] = (part[c % 2, d] + down_in[c, d].astype(jnp.float32)).astype(jnp.bfloat16)
+        down_copy(c, d).start()
+
+    def second_hop(c):
+        @pl.when(z == 2)
+        def _():
+            forward_up(c, 3)
+
+        @pl.when(z == 1)
+        def _():
+            forward_down(c, 0)
+
     def pass_on(c, beside=None):
         for t in (3, 2, 1):
+            d = 3 - t
+
             @pl.when(z == 0)
             def _():
                 if t == 1:
                     up_copy(c, 3).wait_send()
-                elif not start_of_chain(c):
+                elif c > 0:
                     up_copy(c - 1, t - 1).wait_send()
-                up_out[c, t] = part[t].astype(jnp.bfloat16)
+                up_out[c, t] = part[c % 2, t].astype(jnp.bfloat16)
                 up_copy(c, t).start()
-
-            @pl.when((z > 0) & (z < t))
-            def _():
-                arrived(up_in.at[c, t], up_recv.at[c, t])
-                up_out[c, t] = (part[t] + up_in[c, t].astype(jnp.float32)).astype(jnp.bfloat16)
-                up_copy(c, t).start()
-
-            d = 3 - t
 
             @pl.when(z == 3)
             def _():
                 if t == 1:
                     down_copy(c, 0).wait_send()
-                elif not start_of_chain(c):
+                elif c > 0:
                     down_copy(c - 1, d + 1).wait_send()
-                down_out[c, d] = part[d].astype(jnp.bfloat16)
+                down_out[c, d] = part[c % 2, d].astype(jnp.bfloat16)
                 down_copy(c, d).start()
 
-            @pl.when((z < 3) & (z > d))
-            def _():
-                arrived(down_in.at[c, d], down_recv.at[c, d])
-                down_out[c, d] = (part[d] + down_in[c, d].astype(jnp.float32)).astype(jnp.bfloat16)
-                down_copy(c, d).start()
-
+            if t > 1:
+                @pl.when(z == 1)
+                def _():
+                    forward_up(c, t)
+
+                @pl.when(z == 2)
+                def _():
+                    forward_down(c, d)
+
+            if t == 3 and c > 0:
+                second_hop(c - 1)
             if beside is not None:
-                beside(3 - t)
+                beside(d)
 
     def finish(c):
         @pl.when(z > 0)
@@ -462,7 +477,7 @@
         out_ref[:, pl.ds(pl.multiple_of(head * HD, HD), HD)] = (mixed / sums).astype(jnp.bfloat16)
 
     def share_kv(step):
-        if step == 1:
+        if step == 2:
             finish(0)
             kv_all[gy, :, 0:HD] = rotated(final[0, :, 0:HD])
             kv_all[gy, :, HD:] = final[0, :, HD:].astype(jnp.bfloat16)
@@ -471,18 +486,24 @@
     multiply(0, lambda: wkv_ref[kv_rows, :])
     pass_on(0)
     q_chunk(1, share_kv)
-    q_chunk(2, lambda step: kv_forward(step + 1))
-    for step in range(4):
-        source = lax.rem(y_peer + 2 * step, 8)
-        arrived(kv_all.at[source], kv_recv.at[source])
-
-    early = 3 * (chunks - 3)
-
-    def late_chunk(c, carry):
-        q_chunk(c, lambda step: attend((c - 3) * 3 + step))
+    q_chunk(2, lambda step: kv_forward(1) if step == 1 else None)
+    q_chunk(3, lambda step: kv_forward(2 + step // 2) if step != 1 else None)
+
+    def last_beside(step):
+        if step == 0:
+            for s in range(4):
+                source = lax.rem(y_peer + 2 * s, 8)
+                arrived(kv_all.at[source], kv_recv.at[source])
+        attend(step)
+
+    q_chunk(4, last_beside)
+    second_hop(4)
+
+    def late_head(head, carry):
+        attend(head)
         return carry
 
-    lax.fori_loop(3, chunks, late_chunk, 0)
+    lax.fori_loop(3, 6, late_head, 0)
 
     page_len = cache_ref.shape[1]
     pages = slot_ref.shape[1]
@@ -499,11 +520,7 @@
         picked = picked + jnp.dot(chosen, kv_all[s], preferred_element_type=jnp.float32)
     cache_ref[...] = picked.astype(jnp.bfloat16).reshape(cache_ref.shape)
 
-    def late_head(head, carry):
-        attend(head)
-        return carry
-
-    lax.fori_loop(early, 2 * (chunks - 1), late_head, 0)
+    lax.fori_loop(6, 8, late_head, 0)
 
     for copy in sends:
         copy.wait_send()
@@ -565,7 +582,7 @@
             pltpu.VMEM((4, BLK, width), bf16),
             pltpu.VMEM((chunks, BLK, width), bf16),
             pltpu.VMEM((4, BLK, 2 * width), bf16),
-            pltpu.VMEM((4, BLK, BLK), f32),
+            pltpu.VMEM((2, 4, BLK, BLK), f32),
             pltpu.VMEM((chunks, BLK, BLK), f32),
             pltpu.VMEM((chunks, 4, BLK, BLK), bf16),
             pltpu.VMEM((chunks, 4, BLK, BLK), bf16),

time: 117 us -> 92.3 us (0.79)
  Pallas kernels: 112 us -> 87.7 us
    pallas_call x1, Pallas kernels: 112 us -> 87.7 us  [fused(): pl.pallas_call(fused_kernel, out_shape=(jax.ShapeDtypeStruct((BLK, query_...]
where the time goes in v4:
time: 92.3 us; the launch traced here: 92.1 us
  Pallas kernels  87.7 us (95%)
  local copies, waits for them, and re-layouts  3.82 us (4%)
    pallas_call x1, Pallas kernels, fused(): pl.pallas_call(fused_kernel, out_shape=(jax.ShapeDtypeStruct((BLK, query_...  87.7 us
    unnamed x6, local copies, waits for them, and re-layouts  3.24 us

profile of v4, /device:TPU:0, one launch (start us, length us, event | category | flops | bytes accessed | tf_op | source)
XLA Modules:
  0.0 92.1 jit_solution(402170030454052092)
XLA Ops:
  0.6 0.0 copy-start.1
  0.6 0.7 copy-done.1
  1.3 0.6 broadcast_in_dim.11.gain_row
  1.9 87.7 %shard_map.86 = (bf16[256,1024]{1,0:T(8,128)(2,1)}, bf16[16,16,256]{2,1,0:T(8,128)(2,1)}) custom-call(s32[1,8]{1,0:T(1,128)} %bitcast.2, s32[1,128]{1,0:T(1,128)} %bitcast.3, bf16[512,512]{1,0:T(8,128)(2,1)} %hid_ref.1, bf16[1,512]{1,0:T(2,128)(2,1)} %broadcast_in_dim.11.gain_row, f32[1,128]{1,0:T(1,128)} %constant.2.clone.freq_ref, ...), custom_call_target="tpu_custom_call" | custom-call | flops 4000000000 | bytes 8000000 | tf_op jit(solution)/shard_map/pallas_call | solution.py:568
  89.6 0.0 copy-start
  89.6 1.9 %copy.11 = bf16[256,1024]{1,0:T(8,128)(2,1)} copy(bf16[256,1024]{1,0:T(8,128)(2,1)} %get-tuple-element.4) | data formatting | bytes 1048576
  91.5 0.0 copy-done
  91.5 0.7 copy.12
Async XLA Ops:
  0.6 0.7 copy-start.1
  89.6 1.9 %copy-start = (bf16[16,16,256]{2,1,0:T(8,128)(2,1)S(1)}, bf16[16,16,256]{2,1,0:T(8,128)(2,1)}, u32[]{:S(2)}) copy-start(bf16[16,16,256]{2,1,0:T(8,128)(2,1)} %get-tuple-element.5) | copy-start | bytes 393220
